TPU v7x, 32 devices: a whole 2x2x4 slice. The times are simulated.
32 devices in a mesh: sub: 8 (over z, y), mode: 4 (over x, core).
Axes of the slice: x: 2, y: 2, z: 4, core: 2. Of those that a mesh axis runs over, the one named last changes fastest.
Arguments:
- panels: bfloat16 [8, 2048, 768], P('sub', 'mode'), may hold values from -0.59765625 to 0.59765625
- eigvals: float32 [8, 2048], P('sub', 'mode'), may hold values from 0.5 to 20
- counts: int32 [8], P('sub'), may hold values from 512 to 2048, as said below
- separator_diag: float32 [8, 768], P('sub'), may hold values from 4 to 8
- separator_index_tables: int32 [8, 768], replicated, may hold values from 0 to 767, each once within a row
Outputs:
- condensed: float32 [768, 768], P('sub')
Inputs may be any that keep to these rules, and one draw needn't show every extreme that they name: `counts`: every value from 512 to 2048 can occur, and both ends occur in every draw. `separator_index_tables`: each row is a permutation of 0 to 767.
All inputs are finite; a program needn't handle non-finite values.
Results may differ from a plain program's by a relative error of at most 0.0003.
Values sent between devices are 32-bit elements; how exact they have to be, the bound alone decides.
A program may use at most 64 MiB of HBM per device.

v0:
```python
import functools
import math

import jax
import jax.numpy as jnp
from jax import lax
from jax.experimental import pallas as pl
from jax.experimental.pallas import tpu as pltpu
from jax.sharding import PartitionSpec as P

MESH = pl.DeviceIdType.MESH
NT = (((1,), (1,)), ((), ()))
LANES = 128


def plan(subs, modes):
    if subs == 8 and modes == 4:
        x, y, near, far = ("mode", 1), ("sub", 0), ("sub", 1), ("sub", 2)
        return [
            [(True, *x), (True, *y), (True, *near), (True, *far)],
            [(True, *y), (True, *near), (True, *far), (False, *x)],
            [(True, *near), (True, *x), (True, *y), (True, *far)],
        ], 2, 2
    sub_bits, mode_bits = subs.bit_length() - 1, modes.bit_length() - 1
    steps = [(True, "sub", b) for b in range(sub_bits)]
    steps += [(False, "mode", b) for b in range(1, mode_bits)]
    return [steps] * 3, 1, 1


def bit_of(value, bit):
    return (value // 2**bit) % 2


def body(subs, modes, column_parts, pieces, shares, *refs):
    panels_hbm, eig_hbm, counts_ref, diag_hbm, tables_hbm, out_ref = refs[:6]
    panels_ref, eig_ref, diag_ref, tables_ref, load_sems = refs[-5:]
    wt, pt, to_core, from_core, fin, core_sems, fin_sems, send_sems, recv_sems = refs[6:15]
    parts = [part for part in column_parts for _ in range(shares)]
    order = [q * shares + h for h in range(shares) for q in range(len(column_parts))]
    steps = len(parts[0])
    accs = refs[15 : 15 + steps + 1]
    lands = refs[15 + steps + 1 : -5]
    count, chunks = len(parts), len(column_parts)
    loads = [
        pltpu.make_async_copy(source, kept, load_sems.at[i])
        for i, (source, kept) in enumerate(
            [
                (tables_hbm, tables_ref),
                (panels_hbm, panels_ref),
                (eig_hbm, eig_ref),
                (diag_hbm, diag_ref),
            ]
        )
    ]
    for load in loads:
        load.start()
    sub_me, mode_me = lax.axis_index("sub"), lax.axis_index("mode")
    core_me = mode_me % 2
    sep = panels_ref.shape[1]
    depth = panels_ref.shape[0]
    rows = sep // subs // pieces // shares
    place = {"sub": sub_me, "mode": mode_me}

    def partner(axis, bit):
        here = place[axis]
        other = here + 2**bit * (1 - 2 * bit_of(here, bit))
        return (other, mode_me) if axis == "sub" else (sub_me, other)

    sibling = partner("mode", 0)
    links = sorted({step[1:] for part in parts for step in part} | {("mode", 0)})
    barrier = pltpu.get_barrier_semaphore()
    for axis, bit in links:
        pl.semaphore_signal(barrier, inc=1, device_id=partner(axis, bit), device_id_type=MESH)

    first = lax.broadcasted_iota(jnp.int32, (sep, 1), 0)
    across = (sub_me, partner("mode", 1)[1] + 1 - 2 * core_me) if pieces == 2 else None
    greeted = len(links) + (pieces == 2)
    if pieces == 2:
        pl.semaphore_signal(barrier, inc=1, device_id=across, device_id_type=MESH)

    runs = sep // LANES
    place_in_run = lax.broadcasted_iota(jnp.int32, (LANES, sep), 0)
    run_row = lax.broadcasted_iota(jnp.int32, (8, sep), 0)
    run_of = lax.broadcasted_iota(jnp.int32, (8, LANES), 0)
    loads[0].wait()
    index = lax.broadcasted_iota(jnp.int32, (1, sep), 1)
    for level in reversed(range(subs.bit_length() - 1)):
        index = index + 97 * level % sep
        index = jnp.where(index >= sep, index - sep, index)
        line = (sub_me // 2**level) * 2**level + 2**level - 1
        row = tables_ref[pl.ds(line, 1), :]
        table = jnp.zeros((8, LANES), jnp.int32)
        for run in range(runs):
            table = jnp.where(run_of == run, row[:, run * LANES : (run + 1) * LANES], table)
        digits = jnp.concatenate([table // 16, table % 16], axis=0).astype(jnp.float32).astype(jnp.bfloat16)
        mark = jnp.where(place_in_run == index % LANES, 1.0, 0.0).astype(jnp.bfloat16)
        found = jnp.dot(digits, mark, preferred_element_type=jnp.float32)
        value = jnp.where(run_row == index // LANES, found[0:8] * 16.0 + found[8:16], 0.0)
        index = jnp.sum(value, axis=0, keepdims=True).astype(jnp.int32)
    target = jnp.broadcast_to(index, (8, sep)).T[:, 0:1]
    lanes = lax.broadcasted_iota(jnp.int32, (sep, sep), 1)
    moved = jnp.where(target == lanes, 1.0, 0.0).astype(jnp.bfloat16)

    for load in loads[1:]:
        load.wait()
    live = lax.broadcasted_iota(jnp.int32, (1, depth), 1) + mode_me * depth < counts_ref[0]
    scale = jnp.where(live, 1.0, 0.0) / eig_ref[...]
    panels_t = lax.dot_general(moved, panels_ref[...], NT, preferred_element_type=jnp.float32)
    pt[...] = panels_t.astype(jnp.bfloat16)
    wt[...] = (panels_t * scale).astype(jnp.bfloat16)

    diag = diag_ref[...] * jnp.where(mode_me == 0, 1.0, 0.0)
    top = diag.astype(jnp.bfloat16).astype(jnp.float32)
    middle = (diag - top).astype(jnp.bfloat16).astype(jnp.float32)
    low = diag - top - middle
    pick = lax.broadcasted_iota(jnp.int32, (16, sep), 0)
    split = jnp.where(pick == 0, top, jnp.where(pick == 1, middle, jnp.where(pick == 2, low, 0.0)))
    got = lax.dot_general(moved, split.astype(jnp.bfloat16), NT, preferred_element_type=jnp.float32)
    diag_moved = got[:, 0:1] + got[:, 1:2] + got[:, 2:3]
    columns = lax.broadcasted_iota(jnp.int32, (sep, LANES), 1)

    def tile(core, p):
        start = pl.multiple_of((core * chunks + p) * LANES, LANES)
        product = lax.dot_general(
            wt[...], pt[pl.ds(start, LANES), :], NT, preferred_element_type=jnp.float32
        )
        on_diag = columns + start == first
        return jnp.where(on_diag, diag_moved, 0.0) - product

    def slot_of(p, block):
        slot, taken = 0, 0
        for halve, axis, bit in parts[p]:
            if halve:
                if axis == "sub":
                    far = (bit_of(block // pieces, bit) + bit_of(sub_me, bit)) % 2
                else:
                    far = (bit_of(block % pieces, bit - 1) + bit_of(mode_me, bit)) % 2
                    taken = 1
                slot = slot * 2 + far
        return slot if taken else slot * pieces + block % pieces

    def core_copy(p):
        return pltpu.make_async_remote_copy(
            to_core.at[p], from_core.at[p], core_sems.at[0, p], core_sems.at[1, p], sibling, MESH
        )

    blocks = subs * pieces
    def store_tile(kept, core, chunk):
        value = tile(core, chunk)
        for b in range(blocks):
            slot = slot_of(chunk * shares, b)
            for h in range(shares):
                at = (b * shares + h) * rows
                kept[chunk * shares + h, slot, :, :] = value[at : at + rows]

    for chunk in range(chunks):
        store_tile(to_core, 1 - core_me, chunk)
        if chunk == 0:
            pl.semaphore_wait(barrier, greeted)
        for h in range(shares):
            core_copy(chunk * shares + h).start()

    sizes = []
    for p in range(count):
        n, own = blocks, []
        for halve, _, _ in parts[p]:
            n = n // 2 if halve else n
            own.append(n)
        sizes.append(own)

    def exchange(p, k):
        halve, axis, bit = parts[p][k]
        n = sizes[p][k]
        return pltpu.make_async_remote_copy(
            accs[k].at[p, pl.ds(n if halve else 0, n)],
            lands[k].at[p, pl.ds(0, n)],
            send_sems.at[p, k],
            recv_sems.at[p, k],
            partner(axis, bit),
            MESH,
        )

    for chunk in range(chunks):
        store_tile(accs[0], core_me, chunk)
    for p in order:
        core_copy(p).wait_recv()
        accs[0][p] = accs[0][p] + from_core[p]
        exchange(p, 0).start()

    cut = [any(halve and axis == "mode" for halve, axis, _ in part) for part in parts]
    piece_me = bit_of(mode_me, 1)

    def last_copies(p):
        spot = fin.at[core_me, p, pl.ds(piece_me, 1)] if cut[p] else fin.at[core_me, p]
        targets = [sibling, partner("mode", 1), across] if cut[p] else [sibling]
        return [
            pltpu.make_async_remote_copy(spot, spot, fin_sems.at[0, p, i], fin_sems.at[1, p, i], target, MESH)
            for i, target in enumerate(targets)
        ]

    for k in range(steps):
        for p in order:
            n = sizes[p][k]
            exchange(p, k).wait_recv()
            total = accs[k][p, 0:n] + lands[k][p, 0:n]
            if k < steps - 1:
                accs[k + 1][p, 0:n] = total
                exchange(p, k + 1).start()
                continue
            if cut[p]:
                fin[core_me, p, pl.ds(piece_me, 1)] = total
            else:
                fin[core_me, p] = total
            for copy in last_copies(p):
                copy.start()
    for p in order:
        for copy in last_copies(p):
            copy.wait_recv()
    for c in range(2):
        for p in range(count):
            at = (c * chunks + p // shares) * LANES
            for piece in range(pieces):
                down = (piece * shares + p % shares) * rows
                out_ref[down : down + rows, at : at + LANES] = fin[c, p, piece]
    for p in range(count):
        core_copy(p).wait_send()
        for k in range(steps):
            exchange(p, k).wait_send()
        for copy in last_copies(p):
            copy.wait_send()


def solution(mesh):
    subs, modes = mesh.shape["sub"], mesh.shape["mode"]
    column_parts, pieces, shares = plan(subs, modes)
    parts = [part for part in column_parts for _ in range(shares)]

    def local(panels, eigvals, counts, separator_diag, tables):
        sep, depth = panels.shape[2], panels.shape[1]
        own = sep // subs
        rows = own // pieces // shares
        count, steps, blocks = len(parts), len(parts[0]), subs * pieces
        f32 = jnp.float32

        def room(k):
            most = 0
            for part in parts:
                n = blocks
                for halve, _, _ in part[:k]:
                    n = n // 2 if halve else n
                most = max(most, n)
            return pltpu.VMEM((count, most, rows, LANES), f32)

        dma = pltpu.SemaphoreType.DMA
        root = pl.pallas_call(
            functools.partial(body, subs, modes, column_parts, pieces, shares),
            out_shape=jax.ShapeDtypeStruct((own, sep), f32),
            in_specs=[
                pl.BlockSpec(memory_space=pltpu.HBM),
                pl.BlockSpec(memory_space=pltpu.HBM),
                pl.BlockSpec(memory_space=pltpu.SMEM),
                pl.BlockSpec(memory_space=pltpu.HBM),
                pl.BlockSpec(memory_space=pltpu.HBM),
            ],
            out_specs=pl.BlockSpec(memory_space=pltpu.VMEM),
            scratch_shapes=[
                pltpu.VMEM((sep, depth), jnp.bfloat16),
                pltpu.VMEM((sep, depth), jnp.bfloat16),
                pltpu.VMEM((count, blocks, rows, LANES), f32),
                pltpu.VMEM((count, blocks, rows, LANES), f32),
                pltpu.VMEM((2, count, pieces, rows, LANES), f32),
                dma((2, count)),
                dma((2, count, 3)),
                dma((count, steps)),
                dma((count, steps)),
                *[room(k) for k in range(steps + 1)],
                *[room(k + 1) for k in range(steps)],
                pltpu.VMEM((depth, sep), panels.dtype),
                pltpu.VMEM(eigvals.shape, f32),
                pltpu.VMEM(separator_diag.shape, f32),
                pltpu.VMEM(tables.shape, tables.dtype),
                dma((4,)),
            ],
            compiler_params=pltpu.CompilerParams(
                collective_id=0, has_side_effects=True, vmem_limit_bytes=48 * 2**20
            ),
        )(panels[0], eigvals, counts, separator_diag, tables)
        return root * (1.0 / math.sqrt(subs))

    return jax.shard_map(
        local,
        mesh=mesh,
        in_specs=(P("sub", "mode", None), P("sub", "mode"), P("sub"), P("sub", None), P()),
        out_specs=P("sub", None),
        check_vma=False,
    )
```

profile of v0, /device:TPU:0, one launch (start us, length us, event | category | flops | bytes accessed | tf_op | source)
XLA Modules:
  0.0 32.1 jit_solution(3670401613136614131)
XLA Ops:
  0.0 0.0 copy-start.2
  0.7 0.0 copy-done.2
  0.7 0.0 copy-start
  0.7 1.1 %copy-done = bf16[1,512,768]{2,1,0:T(8,128)(2,1)S(1)} copy-done((bf16[1,512,768]{2,1,0:T(8,128)(2,1)S(1)}, bf16[1,512,768]{2,1,0:T(8,128)(2,1)}, u32[]{:S(2)}) %copy-start) | copy-done | bytes 786456
  1.8 0.0 copy-start.1
  1.8 0.7 %copy-done.1 = s32[8,768]{1,0:T(8,128)S(1)} copy-done((s32[8,768]{1,0:T(8,128)S(1)}, s32[8,768]{1,0:T(8,128)}, u32[]{:S(2)}) %copy-start.1) | copy-done | bytes 24600
  2.6 0.0 copy-start.3
  2.6 0.7 %copy-done.3 = f32[1,512]{1,0:T(1,128)S(1)} copy-done((f32[1,512]{1,0:T(1,128)S(1)}, f32[1,512]{1,0:T(1,128)}, u32[]{:S(2)}) %copy-start.3) | copy-done | bytes 2072
  3.2 28.1 %shard_map.55 = f32[96,768]{1,0:T(8,128)S(1)} custom-call(bf16[512,768]{1,0:T(8,128)(2,1)S(1)} %bitcast.1, f32[1,512]{1,0:T(1,128)S(1)} %copy-done.3, s32[1]{0:T(128)S(6)} %copy.6.refs_2_, f32[1,768]{1,0:T(1,128)S(1)} %copy-done.2, s32[8,768]{1,0:T(8,128)S(1)} %copy-done.1), custom_call_target="tpu_custom_call" | custom-call | tf_op jit(solution)/shard_map/pallas_call | solution.py:255
  31.4 0.7 %broadcast_multiply_fusion = f32[96,768]{1,0:T(8,128)} fusion(f32[96,768]{1,0:T(8,128)S(1)} %shard_map.55), kind=kLoop, calls=%fused_computation | loop fusion | flops 73728 | bytes 589824 | tf_op jit(solution)/shard_map/mul | solution.py:288
Async XLA Ops:
  0.0 0.7 %copy-start.2 = (f32[1,768]{1,0:T(1,128)S(1)}, f32[1,768]{1,0:T(1,128)}, u32[]{:S(2)}) copy-start(f32[1,768]{1,0:T(1,128)} %refs_3_.1) | copy-start | bytes 9220
  0.7 1.1 %copy-start = (bf16[1,512,768]{2,1,0:T(8,128)(2,1)S(1)}, bf16[1,512,768]{2,1,0:T(8,128)(2,1)}, u32[]{:S(2)}) copy-start(bf16[1,512,768]{2,1,0:T(8,128)(2,1)} %param.5) | copy-start | bytes 2359300
  1.8 0.7 %copy-start.1 = (s32[8,768]{1,0:T(8,128)S(1)}, s32[8,768]{1,0:T(8,128)}, u32[]{:S(2)}) copy-start(s32[8,768]{1,0:T(8,128)} %refs_4_.1) | copy-start | bytes 73732
  2.6 0.7 %copy-start.3 = (f32[1,512]{1,0:T(1,128)S(1)}, f32[1,512]{1,0:T(1,128)}, u32[]{:S(2)}) copy-start(f32[1,512]{1,0:T(1,128)} %refs_1_.1) | copy-start | bytes 6148
where the time goes:
time: 32.4 us; the launch traced here: 32.1 us
  Pallas kernels  28.1 us (87%)
  local copies, waits for them, and re-layouts  2.57 us (8%)
  other arithmetic  0.74 us (2%)
  between operations  0.68 us (2%)
    pallas_call x1, Pallas kernels, local(): pl.pallas_call(functools.partial(body, subs, modes, column_parts, pieces,...  28.1 us
    unnamed x8, local copies, waits for them, and re-layouts  2.57 us
    mul x1, other arithmetic, local(): return root * (1.0 / math.sqrt(subs))  0.74 us

commit v1 on v0

--- a/solution.py
+++ b/solution.py
@@ -284,7 +284,7 @@
             compiler_params=pltpu.CompilerParams(
                 collective_id=0, has_side_effects=True, vmem_limit_bytes=48 * 2**20
             ),
-        )(panels[0], eigvals, counts, separator_diag, tables)
+        )(*[pltpu.with_memory_space_constraint(a, pltpu.HBM) for a in (panels[0], eigvals)], counts, *[pltpu.with_memory_space_constraint(a, pltpu.HBM) for a in (separator_diag, tables)])
         return root * (1.0 / math.sqrt(subs))
 
     return jax.shard_map(

time: 32.4 us -> 30.3 us (0.935)
  local copies, waits for them, and re-layouts: 2.57 us -> 0 us
  Pallas kernels: 28.1 us -> 28.7 us
    unnamed x8 -> x0, local copies, waits for them, and re-layouts: 2.57 us -> none
    pallas_call x1, Pallas kernels: 28.1 us -> 28.7 us  [local(): pl.pallas_call(functools.partial(body, subs, modes, column_parts, pieces,...]
where the time goes in v1:
time: 30.3 us; the launch traced here: 30.1 us
  Pallas kernels  28.7 us (95%)
  other arithmetic  0.74 us (2%)
  between operations  0.66 us (2%)
    pallas_call x1, Pallas kernels, local(): pl.pallas_call(functools.partial(body, subs, modes, column_parts, pieces,...  28.7 us
    mul x1, other arithmetic, local(): return root * (1.0 / math.sqrt(subs))  0.74 us

profile of v1, /device:TPU:0, one launch (start us, length us, event | category | flops | bytes accessed | tf_op | source)
XLA Modules:
  0.0 30.1 jit_solution(239456116564642921)
XLA Ops:
  0.7 28.7 %shard_map.55 = f32[96,768]{1,0:T(8,128)S(1)} custom-call(bf16[512,768]{1,0:T(8,128)(2,1)} %bitcast.1, f32[1,512]{1,0:T(1,128)} %refs_1_.1, s32[1]{0:T(128)S(6)} %copy.6.refs_2_, f32[1,768]{1,0:T(1,128)} %refs_3_.1, s32[8,768]{1,0:T(8,128)} %refs_4_.1), custom_call_target="tpu_custom_call" | custom-call | tf_op jit(solution)/shard_map/pallas_call | solution.py:255
  29.4 0.7 %broadcast_multiply_fusion = f32[96,768]{1,0:T(8,128)} fusion(f32[96,768]{1,0:T(8,128)S(1)} %shard_map.55), kind=kLoop, calls=%fused_computation | loop fusion | flops 73728 | bytes 589824 | tf_op jit(solution)/shard_map/mul | solution.py:288

commit v2 on v1

v2 whole, which is shorter than its diff:
```python
import functools
import math

import jax
import jax.numpy as jnp
from jax import lax
from jax.experimental import pallas as pl
from jax.experimental.pallas import tpu as pltpu
from jax.sharding import PartitionSpec as P

MESH = pl.DeviceIdType.MESH
NT = (((1,), (1,)), ((), ()))
LANES = 128
CORE = ("mode", 0)
SHARES = 2


def plan(subs, modes):
    if subs == 8 and modes == 4:
        x, y, near, far = ("mode", 1), ("sub", 0), ("sub", 1), ("sub", 2)
        return [
            [("halve", (x,)), ("halve", (y, near)), ("halve", (far,))],
            [("halve", (y,)), ("halve", (x, near)), ("halve", (far,))],
            [("halve", (near,)), ("halve", (x, y)), ("halve", (far,))],
        ], 2, SHARES
    sub_bits, mode_bits = subs.bit_length() - 1, modes.bit_length() - 1
    steps = [("halve", (("sub", b),)) for b in range(sub_bits)]
    steps += [("full", (("mode", b),)) for b in range(1, mode_bits)]
    return [steps] * 3, 1, 1


def halved(phase):
    kind, dims = phase
    return dims if kind == "halve" else ()


def members(dims):
    return [
        (mask, tuple(d for i, d in enumerate(dims) if mask >> (len(dims) - 1 - i) & 1))
        for mask in range(1, 2 ** len(dims))
    ]


def bit_of(value, bit):
    return (value // 2**bit) % 2


def body(subs, modes, column_parts, pieces, shares, *refs):
    panels_hbm, eig_hbm, counts_ref, diag_hbm, tables_hbm, out_ref = refs[:6]
    panels_ref, eig_ref, diag_ref, tables_ref, load_sems = refs[-5:]
    wt, pt, to_core, from_core, fin, core_sems, fin_sems, send_sems, recv_sems = refs[6:15]
    parts = [part for part in column_parts for _ in range(shares)]
    chunks = len(column_parts)
    order = [q * shares + h for h in range(shares) for q in range(chunks)]
    steps = len(parts[0])
    accs = refs[15 : 15 + steps]
    lands = refs[15 + steps : -5]
    count = len(parts)
    loads = [
        pltpu.make_async_copy(source, kept, load_sems.at[i])
        for i, (source, kept) in enumerate(
            [
                (tables_hbm, tables_ref),
                (panels_hbm, panels_ref),
                (eig_hbm, eig_ref),
                (diag_hbm, diag_ref),
            ]
        )
    ]
    for load in loads:
        load.start()
    sub_me, mode_me = lax.axis_index("sub"), lax.axis_index("mode")
    core_me = mode_me % 2
    depth, sep = panels_ref.shape
    rows = sep // subs // pieces // shares
    blocks = subs * pieces
    place = {"sub": sub_me, "mode": mode_me}

    def partner(dims):
        there = dict(place)
        for axis, bit in dims:
            there[axis] = there[axis] + 2**bit * (1 - 2 * bit_of(place[axis], bit))
        return there["sub"], there["mode"]

    gather = [(CORE,)] if pieces == 1 else [(CORE,), (("mode", 1),), (CORE, ("mode", 1))]
    greeted = {tuple(sorted(dims)) for part in parts for _, group in part for _, dims in members(group)}
    greeted = sorted(greeted | set(gather))
    barrier = pltpu.get_barrier_semaphore()
    for dims in greeted:
        pl.semaphore_signal(barrier, inc=1, device_id=partner(dims), device_id_type=MESH)

    runs = sep // LANES
    lane = lax.broadcasted_iota(jnp.int32, (8, LANES), 1)
    run_of = lax.broadcasted_iota(jnp.int32, (8, LANES), 0)

    def look_up(line, at):
        found = jnp.zeros((8, LANES), line.dtype)
        for run in range(runs):
            table = jnp.broadcast_to(line[:, run * LANES : (run + 1) * LANES], (8, LANES))
            here = jnp.take_along_axis(table, at % LANES, axis=1)
            found = jnp.where(at // LANES == run, here, found)
        return found

    loads[0].wait()
    index = run_of * LANES + lane
    for level in reversed(range(subs.bit_length() - 1)):
        index = index + 97 * level % sep
        index = jnp.where(index >= sep, index - sep, index)
        at = (sub_me // 2**level) * 2**level + 2**level - 1
        index = look_up(tables_ref[pl.ds(at, 1), :], index)
    target = jnp.concatenate([index.T[:, run : run + 1] for run in range(runs)], axis=0)
    moved = jnp.where(
        target == lax.broadcasted_iota(jnp.int32, (sep, sep), 1), 1.0, 0.0
    ).astype(jnp.bfloat16)

    for load in loads[1:]:
        load.wait()
    live = lax.broadcasted_iota(jnp.int32, (1, depth), 1) + mode_me * depth < counts_ref[0]
    scale = jnp.where(live, 1.0, 0.0) / eig_ref[...]
    panels_t = lax.dot_general(moved, panels_ref[...], NT, preferred_element_type=jnp.float32)
    pt[...] = panels_t.astype(jnp.bfloat16)
    wt[...] = (panels_t * scale).astype(jnp.bfloat16)
    diag = look_up(diag_ref[...] * jnp.where(mode_me < 2, 1.0, 0.0), index)

    tall = rows * shares
    gathered = tall % 16 == 0
    off_diag = lax.broadcasted_iota(jnp.int32, (tall, LANES), 1) - lax.broadcasted_iota(
        jnp.int32, (tall, LANES), 0
    )

    def block_at(q, slot):
        sub, piece, bit_at = sub_me, bit_of(mode_me, 1) if pieces == 2 else 0, blocks.bit_length() - 2
        for phase in column_parts[q]:
            for axis, bit in halved(phase):
                if slot >> bit_at & 1:
                    if axis == "sub":
                        sub = sub + 2**bit * (1 - 2 * bit_of(sub_me, bit))
                    else:
                        piece = 1 - piece
                bit_at -= 1
        return sub * pieces + piece

    def slot_of(q, block):
        slot = 0
        for phase in column_parts[q]:
            for axis, bit in halved(phase):
                slot = slot * 2 + (block >> bit & 1) + bit_of(sub_me, bit) * (1 - 2 * (block >> bit & 1))
        return slot

    def form(q, slots):
        first = [pl.multiple_of((q * 2 + c) * LANES, LANES) for c in (1 - core_me, core_me)]
        columns = jnp.concatenate([pt[pl.ds(start, LANES), :] for start in first], axis=0)
        if gathered:
            starts = [pl.multiple_of(block_at(q, slot) * tall, 16) for slot in slots]
            left = jnp.concatenate([wt[pl.ds(start, tall), :] for start in starts], axis=0)
        else:
            starts = [block * tall for block in range(blocks)]
            slots = [slot_of(q, block) for block in range(blocks)]
            left = wt[...]
        product = lax.dot_general(left, columns, NT, preferred_element_type=jnp.float32)
        for i, slot in enumerate(slots):
            for h in range(shares):
                at = i * tall + h * rows
                to_core[q * shares + h, slot, :, :] = -product[at : at + rows, 0:LANES]
        mine = jnp.where(core_me == 0, diag[2 * q : 2 * q + 1], diag[2 * q + 1 : 2 * q + 2])
        for i, (slot, start) in enumerate(zip(slots, starts)):
            on_diag = jnp.where(off_diag == start - first[1], mine, 0.0)
            value = on_diag - product[i * tall : (i + 1) * tall, LANES : 2 * LANES]
            for h in range(shares):
                accs[0][q * shares + h, slot, :, :] = value[h * rows : (h + 1) * rows]

    bands = [(blocks // 2, blocks // 2), (0, blocks // 2)] if gathered else [(0, blocks)]

    def core_copy(q, band):
        at, n = bands[band]
        group = pl.ds(q * shares, shares)
        return pltpu.make_async_remote_copy(
            to_core.at[group, pl.ds(at, n)],
            from_core.at[group, pl.ds(at, n)],
            core_sems.at[0, q, band],
            core_sems.at[1, q, band],
            partner((CORE,)),
            MESH,
        )

    sizes = []
    for p in range(count):
        n, own = blocks, []
        for phase in parts[p]:
            n = n >> len(halved(phase))
            own.append(n)
        sizes.append(own)

    def exchange(p, k):
        kind, dims = parts[p][k]
        n = sizes[p][k]
        return [
            pltpu.make_async_remote_copy(
                accs[k].at[p, pl.ds(mask * n if kind == "halve" else 0, n)],
                lands[k].at[p, pl.ds((mask - 1) * n, n)],
                send_sems.at[p, k, mask - 1],
                recv_sems.at[p, k, mask - 1],
                partner(other),
                MESH,
            )
            for mask, other in members(dims)
        ]

    for band, (at, n) in enumerate(bands):
        for q in range(chunks):
            form(q, range(at, at + n))
            if band == 0 and q == 0:
                pl.semaphore_wait(barrier, len(greeted))
            core_copy(q, band).start()
    for band, (at, n) in enumerate(bands):
        for q in range(chunks):
            core_copy(q, band).wait_recv()
            for p in range(q * shares, (q + 1) * shares):
                accs[0][p, at : at + n] = accs[0][p, at : at + n] + from_core[p, at : at + n]
                if band == 0:
                    for copy in exchange(p, 0):
                        copy.start()

    piece_me = bit_of(mode_me, 1)

    def last_copies(p):
        spot = fin.at[core_me, p, pl.ds(piece_me, 1)] if pieces == 2 else fin.at[core_me, p]
        return [
            pltpu.make_async_remote_copy(
                spot, spot, fin_sems.at[0, p, i], fin_sems.at[1, p, i], partner(dims), MESH
            )
            for i, dims in enumerate(gather)
        ]

    for k in range(steps):
        for p in order:
            n = sizes[p][k]
            total = accs[k][p, 0:n]
            for copy in exchange(p, k):
                copy.wait_recv()
            for mask, _ in members(parts[p][k][1]):
                total = total + lands[k][p, (mask - 1) * n : mask * n]
            if k < steps - 1:
                accs[k + 1][p, 0:n] = total
                for copy in exchange(p, k + 1):
                    copy.start()
                continue
            if pieces == 2:
                fin[core_me, p, pl.ds(piece_me, 1)] = total
            else:
                fin[core_me, p] = total
            for copy in last_copies(p):
                copy.start()
    for p in order:
        for copy in last_copies(p):
            copy.wait_recv()
    for c in range(2):
        for p in range(count):
            at = (p // shares * 2 + c) * LANES
            for piece in range(pieces):
                down = (piece * shares + p % shares) * rows
                out_ref[down : down + rows, at : at + LANES] = fin[c, p, piece]
    for q in range(chunks):
        for band in range(len(bands)):
            core_copy(q, band).wait_send()
    for p in range(count):
        for k in range(steps):
            for copy in exchange(p, k):
                copy.wait_send()
        for copy in last_copies(p):
            copy.wait_send()


def solution(mesh):
    subs, modes = mesh.shape["sub"], mesh.shape["mode"]
    column_parts, pieces, shares = plan(subs, modes)
    parts = [part for part in column_parts for _ in range(shares)]

    def local(panels, eigvals, counts, separator_diag, tables):
        sep, depth = panels.shape[2], panels.shape[1]
        own = sep // subs
        rows = own // pieces // shares
        count, steps, blocks = len(parts), len(parts[0]), subs * pieces
        f32 = jnp.float32

        def held(part, k):
            return blocks >> sum(len(halved(phase)) for phase in part[:k])

        def room(k):
            return pltpu.VMEM((count, max(held(part, k) for part in parts), rows, LANES), f32)

        def landing(k):
            most = max((2 ** len(part[k][1]) - 1) * held(part, k + 1) for part in parts)
            return pltpu.VMEM((count, most, rows, LANES), f32)

        most_copies = max(2 ** len(dims) - 1 for part in parts for _, dims in part)
        dma = pltpu.SemaphoreType.DMA
        panels, eigvals, separator_diag, tables = [
            pltpu.with_memory_space_constraint(a, pltpu.HBM)
            for a in (panels[0], eigvals, separator_diag, tables)
        ]
        root = pl.pallas_call(
            functools.partial(body, subs, modes, column_parts, pieces, shares),
            out_shape=jax.ShapeDtypeStruct((own, sep), f32),
            in_specs=[
                pl.BlockSpec(memory_space=pltpu.HBM),
                pl.BlockSpec(memory_space=pltpu.HBM),
                pl.BlockSpec(memory_space=pltpu.SMEM),
                pl.BlockSpec(memory_space=pltpu.HBM),
                pl.BlockSpec(memory_space=pltpu.HBM),
            ],
            out_specs=pl.BlockSpec(memory_space=pltpu.VMEM),
            scratch_shapes=[
                pltpu.VMEM((sep, depth), jnp.bfloat16),
                pltpu.VMEM((sep, depth), jnp.bfloat16),
                pltpu.VMEM((count, blocks, rows, LANES), f32),
                pltpu.VMEM((count, blocks, rows, LANES), f32),
                pltpu.VMEM((2, count, pieces, rows, LANES), f32),
                dma((2, count, 2)),
                dma((2, count, 3)),
                dma((count, steps, most_copies)),
                dma((count, steps, most_copies)),
                *[room(k) for k in range(steps)],
                *[landing(k) for k in range(steps)],
                pltpu.VMEM((depth, sep), panels.dtype),
                pltpu.VMEM(eigvals.shape, f32),
                pltpu.VMEM(separator_diag.shape, f32),
                pltpu.VMEM(tables.shape, tables.dtype),
                dma((4,)),
            ],
            compiler_params=pltpu.CompilerParams(
                collective_id=0, has_side_effects=True, vmem_limit_bytes=48 * 2**20
            ),
        )(panels, eigvals, counts, separator_diag, tables)
        return root * (1.0 / math.sqrt(subs))

    return jax.shard_map(
        local,
        mesh=mesh,
        in_specs=(P("sub", "mode", None), P("sub", "mode"), P("sub"), P("sub", None), P()),
        out_specs=P("sub", None),
        check_vma=False,
    )
```

time: 30.3 us -> 28.6 us (0.944)
  Pallas kernels: 28.7 us -> 27 us
    pallas_call x1, Pallas kernels: 28.7 us -> 27 us  [local(): pl.pallas_call(functools.partial(body, subs, modes, column_parts, pieces,...]
where the time goes in v2:
time: 28.6 us; the launch traced here: 28.4 us
  Pallas kernels  27 us (94%)
  other arithmetic  0.74 us (3%)
  between operations  0.66 us (2%)
    pallas_call x1, Pallas kernels, local(): pl.pallas_call(functools.partial(body, subs, modes, column_parts, pieces,...  27 us
    mul x1, other arithmetic, local(): return root * (1.0 / math.sqrt(subs))  0.74 us

profile of v2, /device:TPU:0, one launch (start us, length us, event | category | flops | bytes accessed | tf_op | source)
XLA Modules:
  0.0 28.4 jit_solution(15703571737489630812)
XLA Ops:
  0.7 27.0 %shard_map.55 = f32[96,768]{1,0:T(8,128)S(1)} custom-call(bf16[512,768]{1,0:T(8,128)(2,1)} %bitcast.1, f32[1,512]{1,0:T(1,128)} %refs_1_.1, s32[1]{0:T(128)S(6)} %copy.6.refs_2_, f32[1,768]{1,0:T(1,128)} %refs_3_.1, s32[8,768]{1,0:T(8,128)} %refs_4_.1), custom_call_target="tpu_custom_call" | custom-call | tf_op jit(solution)/shard_map/pallas_call | solution.py:302
  27.7 0.7 %broadcast_multiply_fusion = f32[96,768]{1,0:T(8,128)} fusion(f32[96,768]{1,0:T(8,128)S(1)} %shard_map.55), kind=kLoop, calls=%fused_computation | loop fusion | flops 73728 | bytes 589824 | tf_op jit(solution)/shard_map/mul | solution.py:335

commit v3 on v2

--- a/solution.py
+++ b/solution.py
@@ -12,7 +12,7 @@
 NT = (((1,), (1,)), ((), ()))
 LANES = 128
 CORE = ("mode", 0)
-SHARES = 2
+SHARES = (24, 24)
 
 
 def plan(subs, modes):
@@ -26,7 +26,7 @@
     sub_bits, mode_bits = subs.bit_length() - 1, modes.bit_length() - 1
     steps = [("halve", (("sub", b),)) for b in range(sub_bits)]
     steps += [("full", (("mode", b),)) for b in range(1, mode_bits)]
-    return [steps] * 3, 1, 1
+    return [steps] * 3, 1, None
 
 
 def halved(phase):
@@ -48,14 +48,12 @@
 def body(subs, modes, column_parts, pieces, shares, *refs):
     panels_hbm, eig_hbm, counts_ref, diag_hbm, tables_hbm, out_ref = refs[:6]
     panels_ref, eig_ref, diag_ref, tables_ref, load_sems = refs[-5:]
-    wt, pt, to_core, from_core, fin, core_sems, fin_sems, send_sems, recv_sems = refs[6:15]
-    parts = [part for part in column_parts for _ in range(shares)]
-    chunks = len(column_parts)
-    order = [q * shares + h for h in range(shares) for q in range(chunks)]
-    steps = len(parts[0])
+    wt, pt, to_core, from_core, fin, core_sems, last_sem, send_sems, recv_sems = refs[6:15]
+    chunks, steps = len(column_parts), len(column_parts[0])
+    spans = [pl.ds(sum(shares[:h]), share) for h, share in enumerate(shares)]
+    order = [(q, h) for h in range(len(shares)) for q in range(chunks)]
     accs = refs[15 : 15 + steps]
     lands = refs[15 + steps : -5]
-    count = len(parts)
     loads = [
         pltpu.make_async_copy(source, kept, load_sems.at[i])
         for i, (source, kept) in enumerate(
@@ -72,7 +70,7 @@
     sub_me, mode_me = lax.axis_index("sub"), lax.axis_index("mode")
     core_me = mode_me % 2
     depth, sep = panels_ref.shape
-    rows = sep // subs // pieces // shares
+    tall = sum(shares)
     blocks = subs * pieces
     place = {"sub": sub_me, "mode": mode_me}
 
@@ -83,7 +81,7 @@
         return there["sub"], there["mode"]
 
     gather = [(CORE,)] if pieces == 1 else [(CORE,), (("mode", 1),), (CORE, ("mode", 1))]
-    greeted = {tuple(sorted(dims)) for part in parts for _, group in part for _, dims in members(group)}
+    greeted = {tuple(sorted(dims)) for part in column_parts for _, group in part for _, dims in members(group)}
     greeted = sorted(greeted | set(gather))
     barrier = pltpu.get_barrier_semaphore()
     for dims in greeted:
@@ -122,7 +120,6 @@
     wt[...] = (panels_t * scale).astype(jnp.bfloat16)
     diag = look_up(diag_ref[...] * jnp.where(mode_me < 2, 1.0, 0.0), index)
 
-    tall = rows * shares
     gathered = tall % 16 == 0
     off_diag = lax.broadcasted_iota(jnp.int32, (tall, LANES), 1) - lax.broadcasted_iota(
         jnp.int32, (tall, LANES), 0
@@ -159,47 +156,45 @@
             left = wt[...]
         product = lax.dot_general(left, columns, NT, preferred_element_type=jnp.float32)
         for i, slot in enumerate(slots):
-            for h in range(shares):
-                at = i * tall + h * rows
-                to_core[q * shares + h, slot, :, :] = -product[at : at + rows, 0:LANES]
+            to_core[q, slot, :, :] = -product[i * tall : (i + 1) * tall, 0:LANES]
         mine = jnp.where(core_me == 0, diag[2 * q : 2 * q + 1], diag[2 * q + 1 : 2 * q + 2])
         for i, (slot, start) in enumerate(zip(slots, starts)):
             on_diag = jnp.where(off_diag == start - first[1], mine, 0.0)
-            value = on_diag - product[i * tall : (i + 1) * tall, LANES : 2 * LANES]
-            for h in range(shares):
-                accs[0][q * shares + h, slot, :, :] = value[h * rows : (h + 1) * rows]
+            accs[0][q, slot, :, :] = on_diag - product[i * tall : (i + 1) * tall, LANES : 2 * LANES]
 
     bands = [(blocks // 2, blocks // 2), (0, blocks // 2)] if gathered else [(0, blocks)]
+
+    def finish(ref, sem):
+        pltpu.make_async_copy(ref, ref, sem).wait()
 
     def core_copy(q, band):
         at, n = bands[band]
-        group = pl.ds(q * shares, shares)
         return pltpu.make_async_remote_copy(
-            to_core.at[group, pl.ds(at, n)],
-            from_core.at[group, pl.ds(at, n)],
-            core_sems.at[0, q, band],
-            core_sems.at[1, q, band],
+            to_core.at[q, pl.ds(at, n)],
+            from_core.at[q, pl.ds(at, n)],
+            send_sems.at[steps],
+            core_sems.at[q, band],
             partner((CORE,)),
             MESH,
         )
 
     sizes = []
-    for p in range(count):
+    for part in column_parts:
         n, own = blocks, []
-        for phase in parts[p]:
+        for phase in part:
             n = n >> len(halved(phase))
             own.append(n)
         sizes.append(own)
 
-    def exchange(p, k):
-        kind, dims = parts[p][k]
-        n = sizes[p][k]
+    def exchange(q, h, k):
+        kind, dims = column_parts[q][k]
+        n = sizes[q][k]
         return [
             pltpu.make_async_remote_copy(
-                accs[k].at[p, pl.ds(mask * n if kind == "halve" else 0, n)],
-                lands[k].at[p, pl.ds((mask - 1) * n, n)],
-                send_sems.at[p, k, mask - 1],
-                recv_sems.at[p, k, mask - 1],
+                accs[k].at[q, pl.ds(mask * n if kind == "halve" else 0, n), spans[h]],
+                lands[k].at[q, pl.ds((mask - 1) * n, n), spans[h]],
+                send_sems.at[k],
+                recv_sems.at[q, h, k],
                 partner(other),
                 MESH,
             )
@@ -215,92 +210,79 @@
     for band, (at, n) in enumerate(bands):
         for q in range(chunks):
             core_copy(q, band).wait_recv()
-            for p in range(q * shares, (q + 1) * shares):
-                accs[0][p, at : at + n] = accs[0][p, at : at + n] + from_core[p, at : at + n]
-                if band == 0:
-                    for copy in exchange(p, 0):
+            accs[0][q, at : at + n] = accs[0][q, at : at + n] + from_core[q, at : at + n]
+            if band == 0:
+                for h in range(len(shares)):
+                    for copy in exchange(q, h, 0):
                         copy.start()
 
-    piece_me = bit_of(mode_me, 1)
-
-    def last_copies(p):
-        spot = fin.at[core_me, p, pl.ds(piece_me, 1)] if pieces == 2 else fin.at[core_me, p]
+    mine = core_me * pieces + (bit_of(mode_me, 1) if pieces == 2 else 0)
+
+    def last_copies(q, h):
+        spot = fin.at[pl.ds(mine, 1), q, spans[h]]
         return [
             pltpu.make_async_remote_copy(
-                spot, spot, fin_sems.at[0, p, i], fin_sems.at[1, p, i], partner(dims), MESH
+                spot, spot, send_sems.at[steps + 1], last_sem, partner(dims), MESH
             )
-            for i, dims in enumerate(gather)
+            for dims in gather
         ]
 
     for k in range(steps):
-        for p in order:
-            n = sizes[p][k]
-            total = accs[k][p, 0:n]
-            for copy in exchange(p, k):
-                copy.wait_recv()
-            for mask, _ in members(parts[p][k][1]):
-                total = total + lands[k][p, (mask - 1) * n : mask * n]
+        for q, h in order:
+            n, span = sizes[q][k], spans[h]
+            total = accs[k][q, 0:n, span]
+            masks = members(column_parts[q][k][1])
+            finish(lands[k].at[q, pl.ds(0, len(masks) * n), span], recv_sems.at[q, h, k])
+            for mask, _ in masks:
+                total = total + lands[k][q, (mask - 1) * n : mask * n, span]
             if k < steps - 1:
-                accs[k + 1][p, 0:n] = total
-                for copy in exchange(p, k + 1):
+                accs[k + 1][q, 0:n, span] = total
+                for copy in exchange(q, h, k + 1):
                     copy.start()
                 continue
-            if pieces == 2:
-                fin[core_me, p, pl.ds(piece_me, 1)] = total
-            else:
-                fin[core_me, p] = total
-            for copy in last_copies(p):
+            fin[pl.ds(mine, 1), q, span] = total
+            for copy in last_copies(q, h):
                 copy.start()
-    for p in order:
-        for copy in last_copies(p):
-            copy.wait_recv()
+    others = fin.at[pl.ds(0, len(gather))]
+    finish(others, last_sem)
     for c in range(2):
-        for p in range(count):
-            at = (p // shares * 2 + c) * LANES
+        for q in range(chunks):
+            at = (q * 2 + c) * LANES
             for piece in range(pieces):
-                down = (piece * shares + p % shares) * rows
-                out_ref[down : down + rows, at : at + LANES] = fin[c, p, piece]
-    for q in range(chunks):
-        for band in range(len(bands)):
-            core_copy(q, band).wait_send()
-    for p in range(count):
-        for k in range(steps):
-            for copy in exchange(p, k):
-                copy.wait_send()
-        for copy in last_copies(p):
-            copy.wait_send()
+                out_ref[piece * tall : (piece + 1) * tall, at : at + LANES] = fin[c * pieces + piece, q]
+    for i, landing in enumerate([*lands, to_core, others]):
+        finish(landing, send_sems.at[i])
 
 
 def solution(mesh):
     subs, modes = mesh.shape["sub"], mesh.shape["mode"]
     column_parts, pieces, shares = plan(subs, modes)
-    parts = [part for part in column_parts for _ in range(shares)]
 
     def local(panels, eigvals, counts, separator_diag, tables):
         sep, depth = panels.shape[2], panels.shape[1]
         own = sep // subs
-        rows = own // pieces // shares
-        count, steps, blocks = len(parts), len(parts[0]), subs * pieces
+        tall = own // pieces
+        cut = shares or (tall,)
+        count, steps, blocks = len(column_parts), len(column_parts[0]), subs * pieces
         f32 = jnp.float32
 
         def held(part, k):
             return blocks >> sum(len(halved(phase)) for phase in part[:k])
 
         def room(k):
-            return pltpu.VMEM((count, max(held(part, k) for part in parts), rows, LANES), f32)
+            return pltpu.VMEM((count, max(held(part, k) for part in column_parts), tall, LANES), f32)
 
         def landing(k):
-            most = max((2 ** len(part[k][1]) - 1) * held(part, k + 1) for part in parts)
-            return pltpu.VMEM((count, most, rows, LANES), f32)
-
-        most_copies = max(2 ** len(dims) - 1 for part in parts for _, dims in part)
+            most = max((2 ** len(part[k][1]) - 1) * held(part, k + 1) for part in column_parts)
+            return pltpu.VMEM((count, most, tall, LANES), f32)
+
         dma = pltpu.SemaphoreType.DMA
         panels, eigvals, separator_diag, tables = [
             pltpu.with_memory_space_constraint(a, pltpu.HBM)
             for a in (panels[0], eigvals, separator_diag, tables)
         ]
         root = pl.pallas_call(
-            functools.partial(body, subs, modes, column_parts, pieces, shares),
+            functools.partial(body, subs, modes, column_parts, pieces, cut),
             out_shape=jax.ShapeDtypeStruct((own, sep), f32),
             in_specs=[
                 pl.BlockSpec(memory_space=pltpu.HBM),
@@ -313,13 +295,13 @@
             scratch_shapes=[
                 pltpu.VMEM((sep, depth), jnp.bfloat16),
                 pltpu.VMEM((sep, depth), jnp.bfloat16),
-                pltpu.VMEM((count, blocks, rows, LANES), f32),
-                pltpu.VMEM((count, blocks, rows, LANES), f32),
-                pltpu.VMEM((2, count, pieces, rows, LANES), f32),
-                dma((2, count, 2)),
-                dma((2, count, 3)),
-                dma((count, steps, most_copies)),
-                dma((count, steps, most_copies)),
+                pltpu.VMEM((count, blocks, tall, LANES), f32),
+                pltpu.VMEM((count, blocks, tall, LANES), f32),
+                pltpu.VMEM((2 * pieces, count, tall, LANES), f32),
+                dma((count, 2)),
+                dma(()),
+                dma((steps + 2,)),
+                dma((count, len(cut), steps)),
                 *[room(k) for k in range(steps)],
                 *[landing(k) for k in range(steps)],
                 pltpu.VMEM((depth, sep), panels.dtype),

time: 28.6 us -> 27.5 us (0.962)
  Pallas kernels: 27 us -> 25.9 us
    pallas_call x1, Pallas kernels: 27 us -> 25.9 us  [local(): pl.pallas_call(functools.partial(body, subs, modes, column_parts, pieces,...]
where the time goes in v3:
time: 27.5 us; the launch traced here: 27.3 us
  Pallas kernels  25.9 us (94%)
  other arithmetic  0.74 us (3%)
  between operations  0.66 us (2%)
    pallas_call x1, Pallas kernels, local(): pl.pallas_call(functools.partial(body, subs, modes, column_parts, pieces,...  25.9 us
    mul x1, other arithmetic, local(): return root * (1.0 / math.sqrt(subs))  0.74 us

profile of v3, /device:TPU:0, one launch (start us, length us, event | category | flops | bytes accessed | tf_op | source)
XLA Modules:
  0.0 27.3 jit_solution(736638262347717961)
XLA Ops:
  0.7 25.9 %shard_map.55 = f32[96,768]{1,0:T(8,128)S(1)} custom-call(bf16[512,768]{1,0:T(8,128)(2,1)} %bitcast.1, f32[1,512]{1,0:T(1,128)} %refs_1_.1, s32[1]{0:T(128)S(6)} %copy.6.refs_2_, f32[1,768]{1,0:T(1,128)} %refs_3_.1, s32[8,768]{1,0:T(8,128)} %refs_4_.1), custom_call_target="tpu_custom_call" | custom-call | tf_op jit(solution)/shard_map/pallas_call | solution.py:284
  26.6 0.7 %broadcast_multiply_fusion = f32[96,768]{1,0:T(8,128)} fusion(f32[96,768]{1,0:T(8,128)S(1)} %shard_map.55), kind=kLoop, calls=%fused_computation | loop fusion | flops 73728 | bytes 589824 | tf_op jit(solution)/shard_map/mul | solution.py:317

commit v4 on v3

--- a/solution.py
+++ b/solution.py
@@ -19,9 +19,9 @@
     if subs == 8 and modes == 4:
         x, y, near, far = ("mode", 1), ("sub", 0), ("sub", 1), ("sub", 2)
         return [
-            [("halve", (x,)), ("halve", (y, near)), ("halve", (far,))],
-            [("halve", (y,)), ("halve", (x, near)), ("halve", (far,))],
-            [("halve", (near,)), ("halve", (x, y)), ("halve", (far,))],
+            [("halve", (x,)), ("halve", (far,y)), ("halve", (near,))],
+            [("halve", (y,)), ("halve", (near,x)), ("halve", (far,))],
+            [("halve", (near,)), ("halve", (y,x)), ("halve", (far,))],
         ], 2, SHARES
     sub_bits, mode_bits = subs.bit_length() - 1, modes.bit_length() - 1
     steps = [("halve", (("sub", b),)) for b in range(sub_bits)]
@@ -154,7 +154,11 @@
             starts = [block * tall for block in range(blocks)]
             slots = [slot_of(q, block) for block in range(blocks)]
             left = wt[...]
-        product = lax.dot_general(left, columns, NT, preferred_element_type=jnp.float32)
+        half = depth // 2
+        product = sum(
+            lax.dot_general(left[:, at : at + half], columns[:, at : at + half], NT, preferred_element_type=jnp.float32)
+            for at in (0, half)
+        )
         for i, slot in enumerate(slots):
             to_core[q, slot, :, :] = -product[i * tall : (i + 1) * tall, 0:LANES]
         mine = jnp.where(core_me == 0, diag[2 * q : 2 * q + 1], diag[2 * q + 1 : 2 * q + 2])

time: 27.5 us -> 27.2 us (0.989)
  no operation moved by 1% of the time
where the time goes in v4:
time: 27.2 us; the launch traced here: 27.1 us
  Pallas kernels  25.7 us (94%)
  other arithmetic  0.74 us (3%)
  between operations  0.66 us (2%)
    pallas_call x1, Pallas kernels, local(): pl.pallas_call(functools.partial(body, subs, modes, column_parts, pieces,...  25.7 us
    mul x1, other arithmetic, local(): return root * (1.0 / math.sqrt(subs))  0.74 us

profile of v4, /device:TPU:0, one launch (start us, length us, event | category | flops | bytes accessed | tf_op | source)
XLA Modules:
  0.0 27.1 jit_solution(16142684501914656175)
XLA Ops:
  0.7 25.7 %shard_map.55 = f32[96,768]{1,0:T(8,128)S(1)} custom-call(bf16[512,768]{1,0:T(8,128)(2,1)} %bitcast.1, f32[1,512]{1,0:T(1,128)} %refs_1_.1, s32[1]{0:T(128)S(6)} %copy.6.refs_2_, f32[1,768]{1,0:T(1,128)} %refs_3_.1, s32[8,768]{1,0:T(8,128)} %refs_4_.1), custom_call_target="tpu_custom_call" | custom-call | tf_op jit(solution)/shard_map/pallas_call | solution.py:288
  26.3 0.7 %broadcast_multiply_fusion = f32[96,768]{1,0:T(8,128)} fusion(f32[96,768]{1,0:T(8,128)S(1)} %shard_map.55), kind=kLoop, calls=%fused_computation | loop fusion | flops 73728 | bytes 589824 | tf_op jit(solution)/shard_map/mul | solution.py:321

commit v5 on v4

--- a/solution.py
+++ b/solution.py
@@ -171,13 +171,17 @@
     def finish(ref, sem):
         pltpu.make_async_copy(ref, ref, sem).wait()
 
-    def core_copy(q, band):
+    whole = pl.ds(0, tall)
+    pieces_out = [(q, 0, h, span) for h, span in enumerate(spans) for q in range(chunks)]
+    pieces_out += [(q, band, 0, whole) for band in range(1, len(bands)) for q in range(chunks)]
+
+    def core_copy(q, band, h, span):
         at, n = bands[band]
         return pltpu.make_async_remote_copy(
-            to_core.at[q, pl.ds(at, n)],
-            from_core.at[q, pl.ds(at, n)],
+            to_core.at[q, pl.ds(at, n), span],
+            from_core.at[q, pl.ds(at, n), span],
             send_sems.at[steps],
-            core_sems.at[q, band],
+            core_sems.at[q, band * len(spans) + h],
             partner((CORE,)),
             MESH,
         )
@@ -208,17 +212,18 @@
     for band, (at, n) in enumerate(bands):
         for q in range(chunks):
             form(q, range(at, at + n))
-            if band == 0 and q == 0:
-                pl.semaphore_wait(barrier, len(greeted))
-            core_copy(q, band).start()
-    for band, (at, n) in enumerate(bands):
-        for q in range(chunks):
-            core_copy(q, band).wait_recv()
-            accs[0][q, at : at + n] = accs[0][q, at : at + n] + from_core[q, at : at + n]
-            if band == 0:
-                for h in range(len(shares)):
-                    for copy in exchange(q, h, 0):
-                        copy.start()
+        if band == 0:
+            pl.semaphore_wait(barrier, len(greeted))
+        for piece in pieces_out:
+            if piece[1] == band:
+                core_copy(*piece).start()
+    for q, band, h, span in pieces_out:
+        at, n = bands[band]
+        core_copy(q, band, h, span).wait_recv()
+        accs[0][q, at : at + n, span] = accs[0][q, at : at + n, span] + from_core[q, at : at + n, span]
+        if band == 0:
+            for copy in exchange(q, h, 0):
+                copy.start()
 
     mine = core_me * pieces + (bit_of(mode_me, 1) if pieces == 2 else 0)
 
@@ -302,7 +307,7 @@
                 pltpu.VMEM((count, blocks, tall, LANES), f32),
                 pltpu.VMEM((count, blocks, tall, LANES), f32),
                 pltpu.VMEM((2 * pieces, count, tall, LANES), f32),
-                dma((count, 2)),
+                dma((count, len(cut) + 1)),
                 dma(()),
                 dma((steps + 2,)),
                 dma((count, len(cut), steps)),

time: 27.2 us -> 26.5 us (0.974)
  Pallas kernels: 25.7 us -> 24.9 us
    pallas_call x1, Pallas kernels: 25.7 us -> 24.9 us  [local(): pl.pallas_call(functools.partial(body, subs, modes, column_parts, pieces,...]
where the time goes in v5:
time: 26.5 us; the launch traced here: 26.3 us
  Pallas kernels  24.9 us (94%)
  other arithmetic  0.74 us (3%)
  between operations  0.66 us (2%)
    pallas_call x1, Pallas kernels, local(): pl.pallas_call(functools.partial(body, subs, modes, column_parts, pieces,...  24.9 us
    mul x1, other arithmetic, local(): return root * (1.0 / math.sqrt(subs))  0.74 us

profile of v5, /device:TPU:0, one launch (start us, length us, event | category | flops | bytes accessed | tf_op | source)
XLA Modules:
  0.0 26.3 jit_solution(17610715185032930348)
XLA Ops:
  0.7 24.9 %shard_map.55 = f32[96,768]{1,0:T(8,128)S(1)} custom-call(bf16[512,768]{1,0:T(8,128)(2,1)} %bitcast.1, f32[1,512]{1,0:T(1,128)} %refs_1_.1, s32[1]{0:T(128)S(6)} %copy.6.refs_2_, f32[1,768]{1,0:T(1,128)} %refs_3_.1, s32[8,768]{1,0:T(8,128)} %refs_4_.1), custom_call_target="tpu_custom_call" | custom-call | tf_op jit(solution)/shard_map/pallas_call | solution.py:293
  25.6 0.7 %broadcast_multiply_fusion = f32[96,768]{1,0:T(8,128)} fusion(f32[96,768]{1,0:T(8,128)S(1)} %shard_map.55), kind=kLoop, calls=%fused_computation | loop fusion | flops 73728 | bytes 589824 | tf_op jit(solution)/shard_map/mul | solution.py:326

commit v6 on v5

--- a/solution.py
+++ b/solution.py
@@ -12,16 +12,16 @@
 NT = (((1,), (1,)), ((), ()))
 LANES = 128
 CORE = ("mode", 0)
-SHARES = (24, 24)
+SHARES = (16, 16, 16)
 
 
 def plan(subs, modes):
     if subs == 8 and modes == 4:
         x, y, near, far = ("mode", 1), ("sub", 0), ("sub", 1), ("sub", 2)
         return [
-            [("halve", (x,)), ("halve", (far,y)), ("halve", (near,))],
-            [("halve", (y,)), ("halve", (near,x)), ("halve", (far,))],
-            [("halve", (near,)), ("halve", (y,x)), ("halve", (far,))],
+            [("halve", (x,)), ("halve", (far, y)), ("dup", (near, x))],
+            [("halve", (y,)), ("halve", (near, x)), ("dup", (far, x))],
+            [("halve", (near,)), ("halve", (y, x)), ("dup", (far, x))],
         ], 2, SHARES
     sub_bits, mode_bits = subs.bit_length() - 1, modes.bit_length() - 1
     steps = [("halve", (("sub", b),)) for b in range(sub_bits)]
@@ -31,7 +31,7 @@
 
 def halved(phase):
     kind, dims = phase
-    return dims if kind == "halve" else ()
+    return {"halve": dims, "full": (), "dup": dims[:1]}[kind]
 
 
 def members(dims):
@@ -80,7 +80,7 @@
             there[axis] = there[axis] + 2**bit * (1 - 2 * bit_of(place[axis], bit))
         return there["sub"], there["mode"]
 
-    gather = [(CORE,)] if pieces == 1 else [(CORE,), (("mode", 1),), (CORE, ("mode", 1))]
+    gather = [(CORE,)]
     greeted = {tuple(sorted(dims)) for part in column_parts for _, group in part for _, dims in members(group)}
     greeted = sorted(greeted | set(gather))
     barrier = pltpu.get_barrier_semaphore()
@@ -161,6 +161,9 @@
         )
         for i, slot in enumerate(slots):
             to_core[q, slot, :, :] = -product[i * tall : (i + 1) * tall, 0:LANES]
+        return lambda: keep(q, slots, starts, first, product)
+
+    def keep(q, slots, starts, first, product):
         mine = jnp.where(core_me == 0, diag[2 * q : 2 * q + 1], diag[2 * q + 1 : 2 * q + 2])
         for i, (slot, start) in enumerate(zip(slots, starts)):
             on_diag = jnp.where(off_diag == start - first[1], mine, 0.0)
@@ -199,7 +202,7 @@
         n = sizes[q][k]
         return [
             pltpu.make_async_remote_copy(
-                accs[k].at[q, pl.ds(mask * n if kind == "halve" else 0, n), spans[h]],
+                accs[k].at[q, pl.ds({"halve": mask, "full": 0, "dup": mask // 2}[kind] * n, n), spans[h]],
                 lands[k].at[q, pl.ds((mask - 1) * n, n), spans[h]],
                 send_sems.at[k],
                 recv_sems.at[q, h, k],
@@ -210,13 +213,14 @@
         ]
 
     for band, (at, n) in enumerate(bands):
-        for q in range(chunks):
-            form(q, range(at, at + n))
+        rest = [form(q, range(at, at + n)) for q in range(chunks)]
         if band == 0:
             pl.semaphore_wait(barrier, len(greeted))
         for piece in pieces_out:
             if piece[1] == band:
                 core_copy(*piece).start()
+        for store in rest:
+            store()
     for q, band, h, span in pieces_out:
         at, n = bands[band]
         core_copy(q, band, h, span).wait_recv()
@@ -226,9 +230,10 @@
                 copy.start()
 
     mine = core_me * pieces + (bit_of(mode_me, 1) if pieces == 2 else 0)
+    there = core_me * pieces + pieces - 1 - (mine - core_me * pieces)
 
     def last_copies(q, h):
-        spot = fin.at[pl.ds(mine, 1), q, spans[h]]
+        spot = fin.at[pl.ds(core_me * pieces, pieces), q, spans[h]]
         return [
             pltpu.make_async_remote_copy(
                 spot, spot, send_sems.at[steps + 1], last_sem, partner(dims), MESH
@@ -242,6 +247,13 @@
             total = accs[k][q, 0:n, span]
             masks = members(column_parts[q][k][1])
             finish(lands[k].at[q, pl.ds(0, len(masks) * n), span], recv_sems.at[q, h, k])
+            if column_parts[q][k][0] == "dup":
+                land = lands[k]
+                fin[pl.ds(mine, 1), q, span] = total + land[q, 1:2, span]
+                fin[pl.ds(there, 1), q, span] = land[q, 0:1, span] + land[q, 2:3, span]
+                for copy in last_copies(q, h):
+                    copy.start()
+                continue
             for mask, _ in masks:
                 total = total + lands[k][q, (mask - 1) * n : mask * n, span]
             if k < steps - 1:
@@ -252,7 +264,7 @@
             fin[pl.ds(mine, 1), q, span] = total
             for copy in last_copies(q, h):
                 copy.start()
-    others = fin.at[pl.ds(0, len(gather))]
+    others = fin.at[pl.ds(0, pieces)]
     finish(others, last_sem)
     for c in range(2):
         for q in range(chunks):

time: 26.5 us -> 25.9 us (0.977)
  Pallas kernels: 24.9 us -> 24.3 us
    pallas_call x1, Pallas kernels: 24.9 us -> 24.3 us  [local(): pl.pallas_call(functools.partial(body, subs, modes, column_parts, pieces,...]
where the time goes in v6:
time: 25.9 us; the launch traced here: 25.7 us
  Pallas kernels  24.3 us (94%)
  other arithmetic  0.74 us (3%)
  between operations  0.66 us (3%)
    pallas_call x1, Pallas kernels, local(): pl.pallas_call(functools.partial(body, subs, modes, column_parts, pieces,...  24.3 us
    mul x1, other arithmetic, local(): return root * (1.0 / math.sqrt(subs))  0.74 us

profile of v6, /device:TPU:0, one launch (start us, length us, event | category | flops | bytes accessed | tf_op | source)
XLA Modules:
  0.0 25.7 jit_solution(16459176423484445506)
XLA Ops:
  0.7 24.3 %shard_map.55 = f32[96,768]{1,0:T(8,128)S(1)} custom-call(bf16[512,768]{1,0:T(8,128)(2,1)} %bitcast.1, f32[1,512]{1,0:T(1,128)} %refs_1_.1, s32[1]{0:T(128)S(6)} %copy.6.refs_2_, f32[1,768]{1,0:T(1,128)} %refs_3_.1, s32[8,768]{1,0:T(8,128)} %refs_4_.1), custom_call_target="tpu_custom_call" | custom-call | tf_op jit(solution)/shard_map/pallas_call | solution.py:305
  25.0 0.7 %broadcast_multiply_fusion = f32[96,768]{1,0:T(8,128)} fusion(f32[96,768]{1,0:T(8,128)S(1)} %shard_map.55), kind=kLoop, calls=%fused_computation | loop fusion | flops 73728 | bytes 589824 | tf_op jit(solution)/shard_map/mul | solution.py:338
